TPU v7x, 32 devices: a whole 2x2x4 slice. The times are simulated.
32 devices in a mesh: row: 8 (over y, x, core), col: 4 (over z).
Axes of the slice: x: 2, y: 2, z: 4, core: 2. Of those that a mesh axis runs over, the one named last changes fastest.
Arguments:
- w_cycle: float32 [2048, 16384], P('col', 'row'), may hold values from -0.125 to 0.125
- amps: float32 [32, 512, 2048], P('col', 'row'), may hold values from -18 to 18
- eps_occ: float32 [32], replicated, may hold values from -3 to -0.3
- eps_vir: float32 [512], replicated, may hold values from 0.3 to 3
- occ_map: int32 [4], replicated, may hold values from 0 to 31
- vir_perm: int32 [512], replicated, may hold values from 0 to 511, each once
Outputs:
- cycle: float32 [16384, 16384], P('row', 'col')
Inputs may be any that keep to these rules, and one draw needn't show every extreme that they name: `occ_map`: each window index names one occupied orbital. `vir_perm`: each virtual orbital appears once.
All inputs are finite; a program needn't handle non-finite values.
Results may differ from a plain program's by a relative error of at most 0.000071.
Values sent between devices are 32-bit elements; how exact they have to be, the bound alone decides.
A program may use at most 192 MiB of HBM per device.

v0:
```python
import jax
import jax.numpy as jnp
from jax import lax
from jax.sharding import PartitionSpec as P


def lookup(indices, table):
    onehot = (indices[:, None] == jnp.arange(table.shape[0], dtype=jnp.int32)[None, :]).astype(
        jnp.float32
    )
    return jnp.dot(
        onehot, table, precision=lax.Precision.HIGHEST, preferred_element_type=jnp.float32
    )


def body(w_cycle, amps, eps_occ, eps_vir, occ_map, vir_perm):
    virtual_count = eps_vir.shape[0]
    j_local = amps.shape[0]
    b_local = amps.shape[1]
    vir_energy = lookup(vir_perm, eps_vir)
    occ_energy = lookup(occ_map, eps_occ)
    pair_energy = (vir_energy[None, :] - occ_energy[:, None]).reshape(-1)
    j_index = jnp.arange(j_local, dtype=jnp.int32) + lax.axis_index("col") * j_local
    j_energy = lookup(j_index, eps_occ)
    b_energy = lax.dynamic_slice_in_dim(vir_energy, lax.axis_index("row") * b_local, b_local)
    denominator = pair_energy[None, None, :] + b_energy[None, :, None] - j_energy[:, None, None]
    scaled = amps / denominator
    w_whole = lax.all_gather(w_cycle, "col", axis=0, tiled=True)
    regrouped = lax.all_to_all(scaled, "row", split_axis=2, concat_axis=1, tiled=True)
    t_columns = regrouped.reshape(j_local * virtual_count, regrouped.shape[2])
    return lax.dot_general(
        w_whole,
        lax.all_gather(t_columns, "row", axis=1, tiled=True),
        (((0,), (1,)), ((), ())),
        precision=lax.Precision.HIGHEST,
        preferred_element_type=jnp.float32,
    )


def solution(mesh):
    placed = (P("col", "row"), P("col", "row", None), P(), P(), P(), P())
    return jax.shard_map(
        body, mesh=mesh, in_specs=placed, out_specs=P("row", "col"), check_vma=False
    )
```

profile of v0, /device:TPU:0, one launch (start us, length us, event | category | flops | bytes accessed | tf_op | source)
XLA Modules:
  0.0 729.4 jit_solution(3464268589470874754)
XLA Ops:
  6.5 0.0 copy-start
  6.5 0.0 all-gather.5.cloned.1.call-start
  6.5 0.7 all-gather.5.cloned.1.call-update
  7.3 0.0 all-gather.3.cloned.1.call-start
  7.3 0.0 copy-done
  7.3 1.3 fusion
  8.6 0.1 dynamic_slice.3
  8.7 0.9 convolution_bitcast_fusion.1
  9.6 0.1 subtract_bitcast_fusion
  9.7 6.9 copy.11
  16.6 0.2 convolution_bitcast_fusion.2
  16.8 0.3 broadcast_add_fusion
  17.1 7.9 %fusion.6 = f32[2048,8,64]{2,1,0:T(8,128)} fusion(f32[8,64,2048]{1,0,2:T(8,128)} %copy.11, f32[8]{0:T(128)S(1)} %convolution_bitcast_fusion.2, f32[64,2048]{0,1:T(8,128)S(1)} %broadcast_add_fusion), kind=kLoop, calls=%fused_computation.16 | loop fusion | flops 2097152 | bytes 8912928
  25.0 10.2 %reshape.65 = f32[8,1,131072]{2,1,0:T(1,128)} reshape(f32[2048,8,64]{2,1,0:T(8,128)} %fusion.6) | data formatting | bytes 8388608
  35.2 54.4 %all_to_all.15 = f32[8,1,131072]{2,1,0:T(1,128)} all-to-all(f32[8,1,131072]{2,1,0:T(1,128)} %reshape.65), channel_id=1, replica_groups=mesh['row'=8,'col'=4] {'row'}, dimensions={0} | all-to-all | bytes 8388608 | tf_op jit(solution)/shard_map/all_to_all | solution.py:29
  89.6 0.5 broadcast.35
  90.1 13.7 %reduce = f32[8,131072]{1,0:T(8,128)} reduce(f32[8,1,131072]{2,1,0:T(1,128)} %all_to_all.15, f32[]{:T(128)} %broadcast.35), dimensions={1}, to_apply=%all_to_all.11.reduce_sub_computation | reduce | bytes 8388612 | tf_op jit(solution)/shard_map/all_to_all | solution.py:29
  103.8 8.9 %reshape.66 = f32[2048,8,64]{2,1,0:T(8,128)} reshape(f32[8,131072]{1,0:T(8,128)} %reduce) | data formatting | bytes 8388608
  112.7 6.8 copy.13
  119.5 0.0 all-gather.3.cloned.1.call-update
  119.6 178.9 %all-gather.5.cloned.1.call-done = f32[2048,2048]{1,0:T(8,128)} async-done(((f32[512,2048]{1,0:T(8,128)}), f32[2048,2048]{1,0:T(8,128)}) %all-gather.5.cloned.1.call-update) | async-done | bytes 16777232 | tf_op jit(solution)/shard_map/all_gather | solution.py:28
  298.4 167.5 %all-gather.3.cloned.1.call-done = f32[4096,2048]{1,0:T(8,128)} async-done(((f32[4096,256]{1,0:T(8,128)}), f32[4096,2048]{1,0:T(8,128)}) %all-gather.3.cloned.1.call-update) | async-done | bytes 33554448 | tf_op jit(solution)/shard_map/all_gather | solution.py:33
  466.0 225.5 %convolution_bitcast_fusion = f32[2048,4096]{0,1:T(8,128)} fusion(f32[4096,2048]{1,0:T(8,128)} %all-gather.3.cloned.1.call-done, f32[2048,2048]{1,0:T(8,128)} %all-gather.5.cloned.1.call-done), kind=kOutput, calls=%fused_computation | convolution fusion | flops 206158430208 | bytes 83886080 | tf_op jit(solution)/shard_map/dot_general | solution.py:31
  691.5 31.1 %copy.14 = f32[2048,4096]{1,0:T(8,128)} copy(f32[2048,4096]{0,1:T(8,128)} %convolution_bitcast_fusion) | data formatting | bytes 67108864 | tf_op jit(solution)/shard_map/dot_general | solution.py:31
  (6 shorter events, 0.0 us)
Async XLA Ops:
  6.5 0.8 copy-start
  6.5 10.1 %copy-start.2 = (f32[32]{0:T(128)S(1)}, f32[32]{0:T(128)}, u32[]{:S(2)}) copy-start(f32[32]{0:T(128)} %param.8) | copy-start | bytes 388
  6.5 291.9 %all-gather.5.cloned.1.call-start = ((), (), s32[]{:S(2)}) async-start(), calls=%async_computation.2 | async-start | bytes 20971520 | tf_op jit(solution)/shard_map/all_gather | solution.py:28
  7.3 458.7 %all-gather.3.cloned.1.call-start = ((), (), s32[]{:S(2)}) async-start(), calls=%async_computation.1 | async-start | bytes 37748736 | tf_op jit(solution)/shard_map/all_gather | solution.py:33
  691.5 31.1 %copy-start.1 = (f32[512]{0:T(512)S(1)}, f32[512]{0:T(512)}, u32[]{:S(2)}) copy-start(f32[512]{0:T(512)} %param.9) | copy-start | bytes 6148
Sparse Core Ops, SparseCore 0:
  8.9 289.4 all-gather.4
  300.3 165.6 all-gather.2
where the time goes:
time: 730 us; the launch traced here: 729 us
  waiting for transfers between devices  347 us (48%)
  matrix products  228 us (31%)
  local copies, waits for them, and re-layouts  64.5 us (9%)
  blocking collectives  54.4 us (7%)
  other arithmetic  22 us (3%)
  between operations  13.4 us (2%)
    dot_general x1, matrix products, body(): lax.dot_general(w_whole, lax.all_gather(t_columns, 'row', axis=1, tiled=T...  226 us
    all_gather x1, waiting for transfers between devices, body(): w_whole = lax.all_gather(w_cycle, 'col', axis=0, tiled=True)  179 us
    all_gather x1, waiting for transfers between devices, body(): lax.all_gather(t_columns, 'row', axis=1, tiled=True)  168 us
    all_to_all x1, blocking collectives, body(): lax.all_to_all(scaled, 'row', split_axis=2, concat_axis=1, tiled=True)  54.4 us
    dot_general x1, local copies, waits for them, and re-layouts, body(): lax.dot_general(w_whole, lax.all_gather(t_columns, 'row', axis=1, tiled=T...  31.1 us
    unnamed x10, local copies, waits for them, and re-layouts  26 us
  transfers between devices with their start and end apart: 2, of which 2 were waited for; matrix products, arithmetic and copies ran while one was open for 8% of the time, Pallas kernels for 0%

commit v1 on v0

v1 whole, which is shorter than its diff:
```python
import functools

import jax
import jax.numpy as jnp
from jax import lax
from jax.experimental import pallas as pl
from jax.experimental.pallas import tpu as pltpu
from jax.sharding import PartitionSpec as P

MESH = pl.DeviceIdType.MESH
LIMIT = 56 * 1024 * 1024


def gather_kernel(amps, whole, own_sem, send, recv):
    me = lax.axis_index("row")
    col = lax.axis_index("col")
    core = lax.rem(me, 2)
    x = lax.rem(me // 2, 2)
    y = me // 4
    sibling = me + 1 - 2 * core
    beside = me + 2 - 4 * x
    across = me + 4 - 8 * y
    corner = beside + across - me
    for peer in (sibling, beside, across):
        pl.semaphore_signal(
            pltpu.get_barrier_semaphore(), inc=1, device_id=(peer, col), device_id_type=MESH
        )
    pl.semaphore_wait(pltpu.get_barrier_semaphore(), 3)

    rows = amps.shape[1]
    js = amps.shape[0]
    half = js // 2

    def slot(owner, first, count):
        return whole.at[pl.ds(first, count), pl.ds(pl.multiple_of(owner * rows, 8), rows), :]

    def remote(k, src, dst, peer):
        copy = pltpu.make_async_remote_copy(
            src_ref=src,
            dst_ref=dst,
            send_sem=send.at[k],
            recv_sem=recv.at[k],
            device_id=(peer, col),
            device_id_type=MESH,
        )
        copy.start()
        return copy

    def forward(k, owner, first, count, peer):
        return remote(k, slot(owner, first, count), slot(owner, first, count), peer)

    to_x = remote(0, amps, slot(me, 0, js), beside)
    to_y = remote(1, amps, slot(me, 0, js), across)
    to_s = remote(2, amps, slot(me, 0, js), sibling)
    own = pltpu.make_async_copy(amps, slot(me, 0, js), own_sem)
    own.start()
    to_x.wait_recv()
    low = forward(3, beside, 0, half, across)
    s_x = forward(4, beside, 0, js, sibling)
    to_y.wait_recv()
    high = forward(5, across, half, js - half, beside)
    s_y = forward(6, across, 0, js, sibling)
    low.wait_recv()
    s_low = forward(7, corner, 0, half, sibling)
    high.wait_recv()
    s_high = forward(8, corner, half, js - half, sibling)
    for copy in (to_s, s_x, s_y, s_low, s_high):
        copy.wait_recv()
    for copy in (to_x, to_y, to_s, low, s_x, high, s_y, s_low, s_high):
        copy.wait_send()
    own.wait()


def gather_amps(amps, row_count):
    js, bs, cks = amps.shape
    return pl.pallas_call(
        gather_kernel,
        out_shape=jax.ShapeDtypeStruct((js, bs * row_count, cks), jnp.float32),
        in_specs=[pl.BlockSpec(memory_space=pl.ANY)],
        out_specs=pl.BlockSpec(memory_space=pl.ANY),
        scratch_shapes=[
            pltpu.SemaphoreType.DMA(()),
            pltpu.SemaphoreType.DMA((9,)),
            pltpu.SemaphoreType.DMA((9,)),
        ],
        compiler_params=pltpu.CompilerParams(
            collective_id=0, has_side_effects=True, vmem_limit_bytes=LIMIT
        ),
        name="gather_amps",
    )(amps)


def scale_kernel(j_energy, amps, pair, b_energy, high, low):
    base = pair[...] + b_energy[...]
    scaled = amps[0] / (base - j_energy[pl.program_id(0)])
    top = scaled.astype(jnp.bfloat16)
    high[0] = top
    low[0] = (scaled - top.astype(jnp.float32)).astype(jnp.bfloat16)


def scale_split(amps, pair, b_energy, j_energy):
    js, bs, cks = amps.shape
    nb = min(bs, 256)
    block = pl.BlockSpec((1, nb, cks), lambda j, b: (j, b, 0))
    shape = jax.ShapeDtypeStruct(amps.shape, jnp.bfloat16)
    return pl.pallas_call(
        scale_kernel,
        grid=(js, bs // nb),
        out_shape=(shape, shape),
        in_specs=[
            pl.BlockSpec(memory_space=pltpu.SMEM),
            block,
            pl.BlockSpec((1, cks), lambda j, b: (0, 0)),
            pl.BlockSpec((nb, 1), lambda j, b: (b, 0)),
        ],
        out_specs=(block, block),
        compiler_params=pltpu.CompilerParams(vmem_limit_bytes=LIMIT),
        cost_estimate=pl.CostEstimate(
            flops=8 * amps.size, bytes_accessed=8 * amps.size, transcendentals=0
        ),
        name="scale_split",
    )(j_energy, amps, pair.reshape(1, cks), b_energy.reshape(bs, 1))


def product_kernel(w, high, low, *rest):
    out, w_high, w_low = rest[-3:]
    cks = w.shape[0]

    @pl.when(pl.program_id(0) == 0)
    def _():
        step = min(cks, 256)

        def turn(i, carry):
            rows = pl.ds(pl.multiple_of(i * step, step), step)
            part = w[rows, :].T
            top = part.astype(jnp.bfloat16)
            w_high[:, rows] = top
            w_low[:, rows] = (part - top.astype(jnp.float32)).astype(jnp.bfloat16)
            return carry

        lax.fori_loop(0, cks // step, turn, 0)

    def dot(a, b):
        return lax.dot_general(
            a, b, (((1,), (1,)), ((), ())), preferred_element_type=jnp.float32
        )

    top = high[...]
    out[...] = (
        dot(w_low[...], top) + dot(w_high[...], low[...])
    ) + dot(w_high[...], top)


def product(w, high, low, out, first, rows_out):
    cks, count = w.shape
    columns = high.shape[0]
    nb = min(columns, 512)
    t_block = pl.BlockSpec((nb, cks), lambda n: (n, 0))
    specs = [pl.BlockSpec((cks, count), lambda n: (0, 0)), t_block, t_block]
    args = [w, high, low]
    aliases = {}
    if out is not None:
        specs.append(pl.BlockSpec(memory_space=pl.ANY))
        args.append(out)
        aliases = {3: 0}
    return pl.pallas_call(
        product_kernel,
        grid=(columns // nb,),
        out_shape=jax.ShapeDtypeStruct((rows_out, columns), jnp.float32),
        in_specs=specs,
        out_specs=pl.BlockSpec((count, nb), lambda n: (first // count, n)),
        scratch_shapes=[
            pltpu.VMEM((count, cks), jnp.bfloat16),
            pltpu.VMEM((count, cks), jnp.bfloat16),
        ],
        input_output_aliases=aliases,
        compiler_params=pltpu.CompilerParams(vmem_limit_bytes=LIMIT),
        cost_estimate=pl.CostEstimate(
            flops=6 * cks * count * columns,
            bytes_accessed=4 * (cks * count + cks * columns + count * columns),
            transcendentals=0,
        ),
        name="product",
    )(*args)


def lookup(indices, table):
    chosen = indices[:, None] == jnp.arange(table.shape[0], dtype=jnp.int32)[None, :]
    return jnp.sum(jnp.where(chosen, table[None, :], 0.0), axis=1)


def body(row_count, w_cycle, amps, eps_occ, eps_vir, occ_map, vir_perm):
    js = amps.shape[0]
    rows_out = w_cycle.shape[1]
    unit = rows_out // 8
    sizes = [2 * unit, 2 * unit, 2 * unit, unit, unit]
    starts = [sum(sizes[:k]) for k in range(len(sizes))]
    gathered = [
        lax.all_gather(w_cycle[:, s : s + n], "col", axis=0, tiled=True)
        for s, n in zip(starts, sizes)
    ]
    vir_energy = lookup(vir_perm, eps_vir)
    occ_energy = lookup(occ_map, eps_occ)
    pair = (vir_energy[None, :] - occ_energy[:, None]).reshape(-1)
    j_energy = lax.dynamic_slice_in_dim(eps_occ, lax.axis_index("col") * js, js)
    if row_count == 8 and js % 2 == 0:
        whole = gather_amps(amps, row_count)
    else:
        whole = lax.all_gather(amps, "row", axis=1, tiled=True)
    high, low = scale_split(whole, pair, vir_energy, j_energy)
    columns = whole.shape[0] * whole.shape[1]
    high = high.reshape(columns, high.shape[2])
    low = low.reshape(columns, low.shape[2])
    out = None
    for s, w in zip(starts, gathered):
        out = product(w, high, low, out, s, rows_out)
    return out


def solution(mesh):
    placed = (P("col", "row"), P("col", "row", None), P(), P(), P(), P())
    return jax.shard_map(
        functools.partial(body, mesh.shape["row"]),
        mesh=mesh,
        in_specs=placed,
        out_specs=P("row", "col"),
        check_vma=False,
    )
```

time: 730 us -> 376 us (0.52)
  Pallas kernels: 0 us -> 325 us
  waiting for transfers between devices: 347 us -> 28.6 us
  matrix products: 228 us -> 0 us
  local copies, waits for them, and re-layouts: 64.5 us -> 7.99 us
  blocking collectives: 54.4 us -> 0 us
  other arithmetic: 22 us -> 0.51 us
    pallas_call x0 -> x7, Pallas kernels: none -> 325 us  [the longest x1 149 us: gather_amps(): pl.pallas_call(gather_kernel, out_shape=jax.ShapeDtypeStruct((js, bs * ro...]
    all_gather x2 -> x5, waiting for transfers between devices: 346 us -> 26.6 us  [body(): lax.all_gather(w_cycle[:, s:s + n], 'col', axis=0, tiled=True)]
    dot_general x4 -> x0, matrix products: 228 us -> none  [the longest x1 226 us: body(): lax.dot_general(w_whole, lax.all_gather(t_columns, 'row', axis=1, tiled=T...]
    all_to_all x1 -> x0, blocking collectives: 54.4 us -> none  [body(): lax.all_to_all(scaled, 'row', split_axis=2, concat_axis=1, tiled=True)]
    dot_general x1 -> x0, local copies, waits for them, and re-layouts: 31.1 us -> none  [body(): lax.dot_general(w_whole, lax.all_gather(t_columns, 'row', axis=1, tiled=T...]
    unnamed x10 -> x9, local copies, waits for them, and re-layouts: 26 us -> 0.62 us
    all_to_all x1 -> x0, other arithmetic: 13.7 us -> none  [body(): lax.all_to_all(scaled, 'row', split_axis=2, concat_axis=1, tiled=True)]
    unnamed x2 -> x1, other arithmetic: 7.96 us -> 0.07 us
  transfers between devices with their start and end apart: 2 -> 5, of which waited for: 2 -> 2; matrix products, arithmetic and copies ran while one was open for 8% -> 1% of each run, Pallas kernels for 0% -> 81%
where the time goes in v1:
time: 376 us
  Pallas kernels  325 us (86%)
  waiting for transfers between devices  28.6 us (8%)
  between operations  13.2 us (4%)
  local copies, waits for them, and re-layouts  7.99 us (2%)
    pallas_call x1, Pallas kernels, gather_amps(): pl.pallas_call(gather_kernel, out_shape=jax.ShapeDtypeStruct((js, bs * ro...  149 us
    pallas_call x5, Pallas kernels, product(): pl.pallas_call(product_kernel, grid=(columns // nb,), out_shape=jax.Shape...  145 us
    pallas_call x1, Pallas kernels, scale_split(): pl.pallas_call(scale_kernel, grid=(js, bs // nb), out_shape=(shape, shape...  31.5 us
    all_gather x5, waiting for transfers between devices, body(): lax.all_gather(w_cycle[:, s:s + n], 'col', axis=0, tiled=True)  26.6 us
  transfers between devices with their start and end apart: 5, of which 2 were waited for; matrix products, arithmetic and copies ran while one was open for 1% of the time, Pallas kernels for 81%

profile of v1, /device:TPU:0, one launch (start us, length us, event | category | flops | bytes accessed | tf_op | source)
XLA Modules:
  0.0 375.8 jit_solution(3577526111070532395)
XLA Ops:
  6.5 3.6 fusion
  10.2 0.0 all-gather.12.cloned.1.call-start
  10.3 0.7 all-gather.12.cloned.1.call-update
  11.0 0.0 all-gather.10.cloned.1.call-start
  11.0 0.7 all-gather.10.cloned.1.call-update
  11.7 0.0 all-gather.8.cloned.1.call-start
  11.7 2.3 fusion.1
  14.1 0.0 all-gather.6.cloned.1.call-start
  14.1 0.5 all-gather.6.cloned.1.call-update
  14.7 0.3 select_reduce_fusion
  14.9 0.8 copy.12.b_energy
  15.8 0.6 dynamic_slice.3.j_energy
  16.4 0.2 select_reduce_fusion.1
  16.6 0.1 subtract_bitcast_fusion
  16.6 0.6 copy.13
  17.2 148.9 %gather_amps.1.amps = f32[8,512,2048]{2,1,0:T(8,128)} custom-call(f32[8,64,2048]{2,1,0:T(8,128)} %amps.1), custom_call_target="tpu_custom_call" | custom-call | tf_op jit(solution)/shard_map/gather_amps/pallas_call | solution.py:76
  166.1 31.5 %scale_split.1 = (bf16[8,512,2048]{2,1,0:T(8,128)(2,1)}, bf16[8,512,2048]{2,1,0:T(8,128)(2,1)}) custom-call(f32[8]{0:T(128)} %dynamic_slice.3.j_energy, f32[8,512,2048]{2,1,0:T(8,128)} %gather_amps.1.amps, f32[1,2048]{1,0:T(1,128)} %bitcast.17, f32[512,1]{1,0:T(8,128)} %copy.12.b_energy), custom_call_target="tpu_custom_call" | custom-call | flops 67108864 | bytes 67108864 | tf_op jit(solution)/shard_map/scale_split/pallas_call | solution.py:106
  197.6 33.9 %product.5.rest_0_ = f32[2048,4096]{1,0:T(8,128)} custom-call(f32[2048,512]{1,0:T(8,128)} %all-gather.14.cloned.1.call-done.w, bf16[4096,2048]{1,0:T(8,128)(2,1)} %bitcast.7, bf16[4096,2048]{1,0:T(8,128)(2,1)} %bitcast.12), custom_call_target="tpu_custom_call" | custom-call | flops 25769803776 | bytes 46137344 | tf_op jit(solution)/shard_map/product/pallas_call | solution.py:166
  231.5 33.9 %product.6.rest_0_ = f32[2048,4096]{1,0:T(8,128)} custom-call(f32[2048,512]{1,0:T(8,128)} %all-gather.12.cloned.1.call-done.w, bf16[4096,2048]{1,0:T(8,128)(2,1)} %bitcast.8, bf16[4096,2048]{1,0:T(8,128)(2,1)} %bitcast.13, f32[2048,4096]{1,0:T(8,128)} %product.5.rest_0_), custom_call_target="tpu_custom_call", output_to_operand_aliasing={{}: (3, {})} | custom-call | flops 25769803776 | bytes 46137344 | tf_op jit(solution)/shard_map/product/pallas_call | solution.py:166
  265.4 33.9 %product.7.rest_0_ = f32[2048,4096]{1,0:T(8,128)} custom-call(f32[2048,512]{1,0:T(8,128)} %all-gather.10.cloned.1.call-done.w, bf16[4096,2048]{1,0:T(8,128)(2,1)} %bitcast.9, bf16[4096,2048]{1,0:T(8,128)(2,1)} %bitcast.14, f32[2048,4096]{1,0:T(8,128)} %product.6.rest_0_), custom_call_target="tpu_custom_call", output_to_operand_aliasing={{}: (3, {})} | custom-call | flops 25769803776 | bytes 46137344 | tf_op jit(solution)/shard_map/product/pallas_call | solution.py:166
  299.3 2.3 all-gather.8.cloned.1.call-done.w
  301.6 21.8 %product.8.rest_0_ = f32[2048,4096]{1,0:T(8,128)} custom-call(f32[2048,256]{1,0:T(8,128)} %all-gather.8.cloned.1.call-done.w, bf16[4096,2048]{1,0:T(8,128)(2,1)} %bitcast.10, bf16[4096,2048]{1,0:T(8,128)(2,1)} %bitcast.15, f32[2048,4096]{1,0:T(8,128)} %product.7.rest_0_), custom_call_target="tpu_custom_call", output_to_operand_aliasing={{}: (3, {})} | custom-call | flops 12884901888 | bytes 39845888 | tf_op jit(solution)/shard_map/product/pallas_call | solution.py:166
  323.3 24.3 %all-gather.6.cloned.1.call-done.w = f32[2048,256]{1,0:T(8,128)} async-done(((f32[512,256]{1,0:T(8,128)}), f32[2048,256]{1,0:T(8,128)}) %all-gather.6.cloned.1.call-update) | async-done | bytes 2097168 | tf_op jit(solution)/shard_map/all_gather | solution.py:199
  347.7 21.6 %product.9 = f32[2048,4096]{1,0:T(8,128)} custom-call(f32[2048,256]{1,0:T(8,128)} %all-gather.6.cloned.1.call-done.w, bf16[4096,2048]{1,0:T(8,128)(2,1)} %bitcast.11, bf16[4096,2048]{1,0:T(8,128)(2,1)} %bitcast.16, f32[2048,4096]{1,0:T(8,128)} %product.8.rest_0_), custom_call_target="tpu_custom_call", output_to_operand_aliasing={{}: (3, {})} | custom-call | flops 12884901888 | bytes 39845888 | tf_op jit(solution)/shard_map/product/pallas_call | solution.py:166
  (14 shorter events, 0.1 us)
Async XLA Ops:
  6.5 191.1 %all-gather.14.cloned.1.call-start = ((), (), s32[]{:S(2)}) async-start(), calls=%async_computation.4 | async-start | bytes 5242880 | tf_op jit(solution)/shard_map/all_gather | solution.py:199
  10.2 4.5 %copy-start = (f32[512]{0:T(512)S(1)}, f32[512]{0:T(512)}, u32[]{:S(2)}) copy-start(f32[512]{0:T(512)} %param.9) | copy-start | bytes 6148
  10.2 4.5 %copy-start.1 = (s32[512]{0:T(512)S(1)}, s32[512]{0:T(512)}, u32[]{:S(2)}) copy-start(s32[512]{0:T(512)} %param.11) | copy-start | bytes 6148
  10.2 5.6 %copy-start.2 = (f32[32]{0:T(128)S(1)}, f32[32]{0:T(128)}, u32[]{:S(2)}) copy-start(f32[32]{0:T(128)} %param.8) | copy-start | bytes 388
  10.2 6.2 %copy-start.3 = (s32[4]{0:T(128)S(1)}, s32[4]{0:T(128)}, u32[]{:S(2)}) copy-start(s32[4]{0:T(128)} %param.10) | copy-start | bytes 52
  10.2 221.3 %all-gather.12.cloned.1.call-start = ((), (), s32[]{:S(2)}) async-start(), calls=%async_computation.3 | async-start | bytes 5242880 | tf_op jit(solution)/shard_map/all_gather | solution.py:199
  11.0 254.4 %all-gather.10.cloned.1.call-start = ((), (), s32[]{:S(2)}) async-start(), calls=%async_computation.2 | async-start | bytes 5242880 | tf_op jit(solution)/shard_map/all_gather | solution.py:199
  11.7 289.9 %all-gather.8.cloned.1.call-start = ((), (), s32[]{:S(2)}) async-start(), calls=%async_computation.1 | async-start | bytes 2621440 | tf_op jit(solution)/shard_map/all_gather | solution.py:199
  14.1 333.6 %all-gather.6.cloned.1.call-start = ((), (), s32[]{:S(2)}) async-start(), calls=%async_computation | async-start | bytes 2621440 | tf_op jit(solution)/shard_map/all_gather | solution.py:199
Sparse Core Ops, SparseCore 0:
  10.3 83.4 all-gather.13
  95.4 79.2 all-gather.11
  176.3 79.2 all-gather.9
  257.1 44.4 all-gather.7
  303.0 44.6 all-gather.5

commit v2 on v1

--- a/solution.py
+++ b/solution.py
@@ -11,7 +11,7 @@
 LIMIT = 56 * 1024 * 1024
 
 
-def gather_kernel(amps, whole, own_sem, send, recv):
+def gather_kernel(cols, amps, w, whole, w_whole, own_sem, send, recv, w_own_sem, w_send, w_recv):
     me = lax.axis_index("row")
     col = lax.axis_index("col")
     core = lax.rem(me, 2)
@@ -25,7 +25,14 @@
         pl.semaphore_signal(
             pltpu.get_barrier_semaphore(), inc=1, device_id=(peer, col), device_id_type=MESH
         )
-    pl.semaphore_wait(pltpu.get_barrier_semaphore(), 3)
+    for d in range(1, cols):
+        pl.semaphore_signal(
+            pltpu.get_barrier_semaphore(),
+            inc=1,
+            device_id=(me, lax.rem(col + d, cols)),
+            device_id_type=MESH,
+        )
+    pl.semaphore_wait(pltpu.get_barrier_semaphore(), 3 + cols - 1)
 
     rows = amps.shape[1]
     js = amps.shape[0]
@@ -54,6 +61,23 @@
     to_s = remote(2, amps, slot(me, 0, js), sibling)
     own = pltpu.make_async_copy(amps, slot(me, 0, js), own_sem)
     own.start()
+    depth = w.shape[0]
+    w_from = w.at[:, pl.ds(0, w_whole.shape[1])]
+    w_slot = w_whole.at[pl.ds(pl.multiple_of(col * depth, 8), depth), :]
+    w_copies = []
+    for d in range(1, cols):
+        copy = pltpu.make_async_remote_copy(
+            src_ref=w_from,
+            dst_ref=w_slot,
+            send_sem=w_send.at[d - 1],
+            recv_sem=w_recv.at[d - 1],
+            device_id=(me, lax.rem(col + d, cols)),
+            device_id_type=MESH,
+        )
+        copy.start()
+        w_copies.append(copy)
+    w_own = pltpu.make_async_copy(w_from, w_slot, w_own_sem)
+    w_own.start()
     to_x.wait_recv()
     low = forward(3, beside, 0, half, across)
     s_x = forward(4, beside, 0, js, sibling)
@@ -69,30 +93,45 @@
     for copy in (to_x, to_y, to_s, low, s_x, high, s_y, s_low, s_high):
         copy.wait_send()
     own.wait()
-
-
-def gather_amps(amps, row_count):
+    for copy in w_copies:
+        copy.wait_recv()
+    for copy in w_copies:
+        copy.wait_send()
+    w_own.wait()
+
+
+def gather_amps(amps, w, count, row_count, cols):
     js, bs, cks = amps.shape
     return pl.pallas_call(
-        gather_kernel,
-        out_shape=jax.ShapeDtypeStruct((js, bs * row_count, cks), jnp.float32),
-        in_specs=[pl.BlockSpec(memory_space=pl.ANY)],
-        out_specs=pl.BlockSpec(memory_space=pl.ANY),
+        functools.partial(gather_kernel, cols),
+        out_shape=(
+            jax.ShapeDtypeStruct((js, bs * row_count, cks), jnp.float32),
+            jax.ShapeDtypeStruct((w.shape[0] * cols, count), jnp.float32),
+        ),
+        in_specs=[pl.BlockSpec(memory_space=pl.ANY)] * 2,
+        out_specs=(pl.BlockSpec(memory_space=pl.ANY),) * 2,
         scratch_shapes=[
             pltpu.SemaphoreType.DMA(()),
             pltpu.SemaphoreType.DMA((9,)),
             pltpu.SemaphoreType.DMA((9,)),
+            pltpu.SemaphoreType.DMA(()),
+            pltpu.SemaphoreType.DMA((cols - 1,)),
+            pltpu.SemaphoreType.DMA((cols - 1,)),
         ],
         compiler_params=pltpu.CompilerParams(
             collective_id=0, has_side_effects=True, vmem_limit_bytes=LIMIT
         ),
         name="gather_amps",
-    )(amps)
+    )(amps, w)
 
 
 def scale_kernel(j_energy, amps, pair, b_energy, high, low):
     base = pair[...] + b_energy[...]
-    scaled = amps[0] / (base - j_energy[pl.program_id(0)])
+    denominator = base - j_energy[pl.program_id(0)]
+    inverse = pl.reciprocal(denominator, approx=True)
+    inverse = inverse * (2.0 - denominator * inverse)
+    inverse = inverse + inverse * (1.0 - denominator * inverse)
+    scaled = amps[0] * inverse
     top = scaled.astype(jnp.bfloat16)
     high[0] = top
     low[0] = (scaled - top.astype(jnp.float32)).astype(jnp.bfloat16)
@@ -122,9 +161,11 @@
     )(j_energy, amps, pair.reshape(1, cks), b_energy.reshape(bs, 1))
 
 
-def product_kernel(w, high, low, *rest):
-    out, w_high, w_low = rest[-3:]
-    cks = w.shape[0]
+def product_kernel(parts, *refs):
+    ws = refs[:parts]
+    high, low = refs[parts : parts + 2]
+    out, w_high, w_low = refs[-3:]
+    cks, count = ws[0].shape
 
     @pl.when(pl.program_id(0) == 0)
     def _():
@@ -132,10 +173,12 @@
 
         def turn(i, carry):
             rows = pl.ds(pl.multiple_of(i * step, step), step)
-            part = w[rows, :].T
-            top = part.astype(jnp.bfloat16)
-            w_high[:, rows] = top
-            w_low[:, rows] = (part - top.astype(jnp.float32)).astype(jnp.bfloat16)
+            for k, w in enumerate(ws):
+                part = w[rows, :].T
+                top = part.astype(jnp.bfloat16)
+                at = pl.ds(k * count, count)
+                w_high[at, rows] = top
+                w_low[at, rows] = (part - top.astype(jnp.float32)).astype(jnp.bfloat16)
             return carry
 
         lax.fori_loop(0, cks // step, turn, 0)
@@ -151,20 +194,22 @@
     ) + dot(w_high[...], top)
 
 
-def product(w, high, low, out, first, rows_out):
-    cks, count = w.shape
+def product(ws, high, low, out, first, rows_out):
+    cks, each = ws[0].shape
+    count = each * len(ws)
     columns = high.shape[0]
     nb = min(columns, 512)
     t_block = pl.BlockSpec((nb, cks), lambda n: (n, 0))
-    specs = [pl.BlockSpec((cks, count), lambda n: (0, 0)), t_block, t_block]
-    args = [w, high, low]
+    w_block = pl.BlockSpec((cks, each), lambda n: (0, 0), pipeline_mode=pl.Buffered(1))
+    specs = [w_block] * len(ws) + [t_block, t_block]
+    args = [*ws, high, low]
     aliases = {}
     if out is not None:
         specs.append(pl.BlockSpec(memory_space=pl.ANY))
         args.append(out)
-        aliases = {3: 0}
+        aliases = {len(ws) + 2: 0}
     return pl.pallas_call(
-        product_kernel,
+        functools.partial(product_kernel, len(ws)),
         grid=(columns // nb,),
         out_shape=jax.ShapeDtypeStruct((rows_out, columns), jnp.float32),
         in_specs=specs,
@@ -189,38 +234,41 @@
     return jnp.sum(jnp.where(chosen, table[None, :], 0.0), axis=1)
 
 
-def body(row_count, w_cycle, amps, eps_occ, eps_vir, occ_map, vir_perm):
+def body(row_count, col_count, w_cycle, amps, eps_occ, eps_vir, occ_map, vir_perm):
     js = amps.shape[0]
     rows_out = w_cycle.shape[1]
     unit = rows_out // 8
+    direct = row_count == 8 and js % 2 == 0
     sizes = [2 * unit, 2 * unit, 2 * unit, unit, unit]
     starts = [sum(sizes[:k]) for k in range(len(sizes))]
     gathered = [
-        lax.all_gather(w_cycle[:, s : s + n], "col", axis=0, tiled=True)
+        None
+        if direct and s == 0
+        else lax.all_gather(w_cycle[:, s : s + n], "col", axis=0, tiled=True)
         for s, n in zip(starts, sizes)
     ]
     vir_energy = lookup(vir_perm, eps_vir)
     occ_energy = lookup(occ_map, eps_occ)
     pair = (vir_energy[None, :] - occ_energy[:, None]).reshape(-1)
     j_energy = lax.dynamic_slice_in_dim(eps_occ, lax.axis_index("col") * js, js)
-    if row_count == 8 and js % 2 == 0:
-        whole = gather_amps(amps, row_count)
+    if direct:
+        whole, gathered[0] = gather_amps(amps, w_cycle, sizes[0], row_count, col_count)
     else:
         whole = lax.all_gather(amps, "row", axis=1, tiled=True)
     high, low = scale_split(whole, pair, vir_energy, j_energy)
     columns = whole.shape[0] * whole.shape[1]
     high = high.reshape(columns, high.shape[2])
     low = low.reshape(columns, low.shape[2])
-    out = None
-    for s, w in zip(starts, gathered):
-        out = product(w, high, low, out, s, rows_out)
+    out = product(gathered[:2], high, low, None, 0, rows_out)
+    for s, w in zip(starts[2:], gathered[2:]):
+        out = product([w], high, low, out, s, rows_out)
     return out
 
 
 def solution(mesh):
     placed = (P("col", "row"), P("col", "row", None), P(), P(), P(), P())
     return jax.shard_map(
-        functools.partial(body, mesh.shape["row"]),
+        functools.partial(body, mesh.shape["row"], mesh.shape["col"]),
         mesh=mesh,
         in_specs=placed,
         out_specs=P("row", "col"),

time: 376 us -> 373 us (level)
  waiting for transfers between devices: 28.6 us -> 8.04 us
  Pallas kernels: 325 us -> 344 us
    all_gather x5 -> x4, waiting for transfers between devices: 26.6 us -> 6.79 us  [body(): lax.all_gather(w_cycle[:, s:s + n], 'col', axis=0, tiled=True)]
    pallas_call x6 -> x5, Pallas kernels: 294 us -> 305 us  [the longest x1 165 us: gather_amps(): pl.pallas_call(functools.partial(gather_kernel, cols), out_shape=(jax.Sha...]
    pallas_call x1, Pallas kernels: 31.5 us -> 38.6 us  [scale_split(): pl.pallas_call(scale_kernel, grid=(js, bs // nb), out_shape=(shape, shape...]
  transfers between devices with their start and end apart: 5 -> 4, of which waited for: 2 -> 1; matrix products, arithmetic and copies ran while one was open for 1% -> 1% of each run, Pallas kernels for 81% -> 86%
where the time goes in v2:
time: 373 us
  Pallas kernels  344 us (92%)
  between operations  13.2 us (4%)
  waiting for transfers between devices  8.04 us (2%)
  local copies, waits for them, and re-layouts  7.45 us (2%)
    pallas_call x1, Pallas kernels, gather_amps(): pl.pallas_call(functools.partial(gather_kernel, cols), out_shape=(jax.Sha...  165 us
    pallas_call x4, Pallas kernels, product(): pl.pallas_call(functools.partial(product_kernel, len(ws)), grid=(columns...  140 us
    pallas_call x1, Pallas kernels, scale_split(): pl.pallas_call(scale_kernel, grid=(js, bs // nb), out_shape=(shape, shape...  38.6 us
  transfers between devices with their start and end apart: 4, of which 1 were waited for; matrix products, arithmetic and copies ran while one was open for 1% of the time, Pallas kernels for 86%

profile of v2, /device:TPU:0, one launch (start us, length us, event | category | flops | bytes accessed | tf_op | source)
XLA Modules:
  0.0 372.9 jit_solution(17200787843232025681)
XLA Ops:
  6.5 3.0 fusion
  9.6 0.0 all-gather.11.cloned.1.call-update
  9.6 0.0 all-gather.9.cloned.1.call-start
  9.6 0.7 all-gather.9.cloned.1.call-update
  10.4 0.0 all-gather.7.cloned.1.call-start
  10.4 2.3 fusion.1
  12.7 0.0 all-gather.7.cloned.1.call-update
  12.7 0.0 all-gather.5.cloned.1.call-start
  12.8 0.5 all-gather.5.cloned.1.call-update
  13.3 0.0 copy-start.1
  13.3 0.0 copy-start.2
  13.4 165.3 %gather_amps.1 = (f32[8,512,2048]{2,1,0:T(8,128)}, f32[2048,512]{1,0:T(8,128)}) custom-call(f32[8,64,2048]{2,1,0:T(8,128)} %amps.1, f32[512,2048]{1,0:T(8,128)} %w.1), custom_call_target="tpu_custom_call" | custom-call | tf_op jit(solution)/shard_map/gather_amps/pallas_call | solution.py:105
  178.7 0.2 select_reduce_fusion
  178.9 0.9 copy.11.b_energy
  179.8 0.6 dynamic_slice.3.j_energy
  180.4 0.2 select_reduce_fusion.1
  180.6 0.1 subtract_bitcast_fusion
  180.7 0.6 copy.12
  181.3 38.6 %scale_split.1 = (bf16[8,512,2048]{2,1,0:T(8,128)(2,1)}, bf16[8,512,2048]{2,1,0:T(8,128)(2,1)}) custom-call(f32[8]{0:T(128)} %dynamic_slice.3.j_energy, f32[8,512,2048]{2,1,0:T(8,128)} %get-tuple-element.9.amps, f32[1,2048]{1,0:T(1,128)} %bitcast.15, f32[512,1]{1,0:T(8,128)} %copy.11.b_energy), custom_call_target="tpu_custom_call" | custom-call | flops 67108864 | bytes 67108864 | tf_op jit(solution)/shard_map/scale_split/pallas_call | solution.py:145
  219.8 62.6 %product.4.refs_3_ = f32[2048,4096]{1,0:T(8,128)} custom-call(f32[2048,512]{1,0:T(8,128)} %get-tuple-element.12.refs_0_, f32[2048,512]{1,0:T(8,128)} %all-gather.11.cloned.1.call-done.refs_1_, bf16[4096,2048]{1,0:T(8,128)(2,1)} %bitcast.7, bf16[4096,2048]{1,0:T(8,128)(2,1)} %bitcast.11), custom_call_target="tpu_custom_call" | custom-call | flops 51539607552 | bytes 58720256 | tf_op jit(solution)/shard_map/product/pallas_call | solution.py:211
  282.5 33.9 %product.5.refs_3_ = f32[2048,4096]{1,0:T(8,128)} custom-call(f32[2048,512]{1,0:T(8,128)} %all-gather.9.cloned.1.call-done.refs_0_, bf16[4096,2048]{1,0:T(8,128)(2,1)} %bitcast.8, bf16[4096,2048]{1,0:T(8,128)(2,1)} %bitcast.12, f32[2048,4096]{1,0:T(8,128)} %product.4.refs_3_), custom_call_target="tpu_custom_call", output_to_operand_aliasing={{}: (3, {})} | custom-call | flops 25769803776 | bytes 46137344 | tf_op jit(solution)/shard_map/product/pallas_call | solution.py:211
  316.4 21.7 %product.6.refs_3_ = f32[2048,4096]{1,0:T(8,128)} custom-call(f32[2048,256]{1,0:T(8,128)} %all-gather.7.cloned.1.call-done.refs_0_, bf16[4096,2048]{1,0:T(8,128)(2,1)} %bitcast.9, bf16[4096,2048]{1,0:T(8,128)(2,1)} %bitcast.13, f32[2048,4096]{1,0:T(8,128)} %product.5.refs_3_), custom_call_target="tpu_custom_call", output_to_operand_aliasing={{}: (3, {})} | custom-call | flops 12884901888 | bytes 39845888 | tf_op jit(solution)/shard_map/product/pallas_call | solution.py:211
  338.1 6.8 %all-gather.5.cloned.1.call-done.refs_0_ = f32[2048,256]{1,0:T(8,128)} async-done(((f32[512,256]{1,0:T(8,128)}), f32[2048,256]{1,0:T(8,128)}) %all-gather.5.cloned.1.call-update) | async-done | bytes 2097168 | tf_op jit(solution)/shard_map/all_gather | solution.py:247
  344.9 21.6 %product.7 = f32[2048,4096]{1,0:T(8,128)} custom-call(f32[2048,256]{1,0:T(8,128)} %all-gather.5.cloned.1.call-done.refs_0_, bf16[4096,2048]{1,0:T(8,128)(2,1)} %bitcast.10, bf16[4096,2048]{1,0:T(8,128)(2,1)} %bitcast.14, f32[2048,4096]{1,0:T(8,128)} %product.6.refs_3_), custom_call_target="tpu_custom_call", output_to_operand_aliasing={{}: (3, {})} | custom-call | flops 12884901888 | bytes 39845888 | tf_op jit(solution)/shard_map/product/pallas_call | solution.py:211
  (10 shorter events, 0.0 us)
Async XLA Ops:
  6.5 213.3 %all-gather.11.cloned.1.call-start = ((), (), s32[]{:S(2)}) async-start(), calls=%async_computation.3 | async-start | bytes 5242880 | tf_op jit(solution)/shard_map/all_gather | solution.py:247
  9.6 272.9 %all-gather.9.cloned.1.call-start = ((), (), s32[]{:S(2)}) async-start(), calls=%async_computation.2 | async-start | bytes 5242880 | tf_op jit(solution)/shard_map/all_gather | solution.py:247
  10.4 306.0 %all-gather.7.cloned.1.call-start = ((), (), s32[]{:S(2)}) async-start(), calls=%async_computation.1 | async-start | bytes 2621440 | tf_op jit(solution)/shard_map/all_gather | solution.py:247
  12.7 332.1 %all-gather.5.cloned.1.call-start = ((), (), s32[]{:S(2)}) async-start(), calls=%async_computation | async-start | bytes 2621440 | tf_op jit(solution)/shard_map/all_gather | solution.py:247
  13.3 165.3 %copy-start = (f32[512]{0:T(512)S(1)}, f32[512]{0:T(512)}, u32[]{:S(2)}) copy-start(f32[512]{0:T(512)} %param.9) | copy-start | bytes 6148
  13.3 165.3 %copy-start.1 = (s32[512]{0:T(512)S(1)}, s32[512]{0:T(512)}, u32[]{:S(2)}) copy-start(s32[512]{0:T(512)} %param.11) | copy-start | bytes 6148
  13.3 166.4 %copy-start.2 = (f32[32]{0:T(128)S(1)}, f32[32]{0:T(128)}, u32[]{:S(2)}) copy-start(f32[32]{0:T(128)} %param.8) | copy-start | bytes 388
  13.3 167.0 %copy-start.3 = (s32[4]{0:T(128)S(1)}, s32[4]{0:T(128)}, u32[]{:S(2)}) copy-start(s32[4]{0:T(128)} %param.10) | copy-start | bytes 52
Sparse Core Ops, SparseCore 0:
  9.7 157.4 all-gather.10
  168.8 83.8 all-gather.8
  254.2 44.4 all-gather.6
  300.2 44.6 all-gather.4

commit v3 on v1

--- a/solution.py
+++ b/solution.py
@@ -90,40 +90,14 @@
     )(amps)
 
 
-def scale_kernel(j_energy, amps, pair, b_energy, high, low):
-    base = pair[...] + b_energy[...]
-    scaled = amps[0] / (base - j_energy[pl.program_id(0)])
-    top = scaled.astype(jnp.bfloat16)
-    high[0] = top
-    low[0] = (scaled - top.astype(jnp.float32)).astype(jnp.bfloat16)
-
-
-def scale_split(amps, pair, b_energy, j_energy):
-    js, bs, cks = amps.shape
-    nb = min(bs, 256)
-    block = pl.BlockSpec((1, nb, cks), lambda j, b: (j, b, 0))
-    shape = jax.ShapeDtypeStruct(amps.shape, jnp.bfloat16)
-    return pl.pallas_call(
-        scale_kernel,
-        grid=(js, bs // nb),
-        out_shape=(shape, shape),
-        in_specs=[
-            pl.BlockSpec(memory_space=pltpu.SMEM),
-            block,
-            pl.BlockSpec((1, cks), lambda j, b: (0, 0)),
-            pl.BlockSpec((nb, 1), lambda j, b: (b, 0)),
-        ],
-        out_specs=(block, block),
-        compiler_params=pltpu.CompilerParams(vmem_limit_bytes=LIMIT),
-        cost_estimate=pl.CostEstimate(
-            flops=8 * amps.size, bytes_accessed=8 * amps.size, transcendentals=0
-        ),
-        name="scale_split",
-    )(j_energy, amps, pair.reshape(1, cks), b_energy.reshape(bs, 1))
-
-
-def product_kernel(w, high, low, *rest):
-    out, w_high, w_low = rest[-3:]
+def product_kernel(first, w, *refs):
+    if first:
+        t, out, high, low, w_high, w_low = refs
+        top = t[...].astype(jnp.bfloat16)
+        high[...] = top
+        low[...] = (t[...] - top.astype(jnp.float32)).astype(jnp.bfloat16)
+    else:
+        high, low, _, out, w_high, w_low = refs
     cks = w.shape[0]
 
     @pl.when(pl.program_id(0) == 0)
@@ -151,24 +125,31 @@
     ) + dot(w_high[...], top)
 
 
-def product(w, high, low, out, first, rows_out):
+def product(w, t, out, start, rows_out):
     cks, count = w.shape
-    columns = high.shape[0]
+    columns = t[0].shape[0]
     nb = min(columns, 512)
+    first = out is None
     t_block = pl.BlockSpec((nb, cks), lambda n: (n, 0))
-    specs = [pl.BlockSpec((cks, count), lambda n: (0, 0)), t_block, t_block]
-    args = [w, high, low]
+    w_block = pl.BlockSpec((cks, count), lambda n: (0, 0), pipeline_mode=pl.Buffered(1))
+    shapes = [jax.ShapeDtypeStruct((rows_out, columns), jnp.float32)]
+    outs = [pl.BlockSpec((count, nb), lambda n: (start // count, n))]
+    specs = [w_block] + [t_block] * len(t)
+    args = [w, *t]
     aliases = {}
-    if out is not None:
+    if first:
+        shapes += [jax.ShapeDtypeStruct((columns, cks), jnp.bfloat16)] * 2
+        outs += [t_block] * 2
+    else:
         specs.append(pl.BlockSpec(memory_space=pl.ANY))
         args.append(out)
         aliases = {3: 0}
     return pl.pallas_call(
-        product_kernel,
+        functools.partial(product_kernel, first),
         grid=(columns // nb,),
-        out_shape=jax.ShapeDtypeStruct((rows_out, columns), jnp.float32),
+        out_shape=shapes,
         in_specs=specs,
-        out_specs=pl.BlockSpec((count, nb), lambda n: (first // count, n)),
+        out_specs=outs,
         scratch_shapes=[
             pltpu.VMEM((count, cks), jnp.bfloat16),
             pltpu.VMEM((count, cks), jnp.bfloat16),
@@ -193,8 +174,8 @@
     js = amps.shape[0]
     rows_out = w_cycle.shape[1]
     unit = rows_out // 8
-    sizes = [2 * unit, 2 * unit, 2 * unit, unit, unit]
-    starts = [sum(sizes[:k]) for k in range(len(sizes))]
+    sizes = [4 * unit, 3 * unit, unit]
+    starts = [4 * unit, 0, 3 * unit]
     gathered = [
         lax.all_gather(w_cycle[:, s : s + n], "col", axis=0, tiled=True)
         for s, n in zip(starts, sizes)
@@ -203,17 +184,19 @@
     occ_energy = lookup(occ_map, eps_occ)
     pair = (vir_energy[None, :] - occ_energy[:, None]).reshape(-1)
     j_energy = lax.dynamic_slice_in_dim(eps_occ, lax.axis_index("col") * js, js)
+    bs = amps.shape[1]
+    b_energy = lax.dynamic_slice_in_dim(vir_energy, lax.axis_index("row") * bs, bs)
+    denominator = pair[None, None, :] + b_energy[None, :, None] - j_energy[:, None, None]
+    scaled = amps / denominator
     if row_count == 8 and js % 2 == 0:
-        whole = gather_amps(amps, row_count)
+        whole = gather_amps(scaled, row_count)
     else:
-        whole = lax.all_gather(amps, "row", axis=1, tiled=True)
-    high, low = scale_split(whole, pair, vir_energy, j_energy)
+        whole = lax.all_gather(scaled, "row", axis=1, tiled=True)
     columns = whole.shape[0] * whole.shape[1]
-    high = high.reshape(columns, high.shape[2])
-    low = low.reshape(columns, low.shape[2])
-    out = None
-    for s, w in zip(starts, gathered):
-        out = product(w, high, low, out, s, rows_out)
+    whole = whole.reshape(columns, whole.shape[2])
+    out, high, low = product(gathered[0], [whole], None, starts[0], rows_out)
+    for s, w in zip(starts[1:], gathered[1:]):
+        (out,) = product(w, [high, low], out, s, rows_out)
     return out
 
 

time: 376 us -> 354 us (0.941)
  Pallas kernels: 325 us -> 287 us
  waiting for transfers between devices: 28.6 us -> 39.6 us
  other arithmetic: 0.51 us -> 5.8 us
    pallas_call x6 -> x3, Pallas kernels: 176 us -> 138 us  [product(): pl.pallas_call(functools.partial(product_kernel, first), grid=(columns //...]
    all_gather x5 -> x3, waiting for transfers between devices: 26.6 us -> 39.6 us  [body(): lax.all_gather(w_cycle[:, s:s + n], 'col', axis=0, tiled=True)]
    div x0 -> x1, other arithmetic: none -> 5.19 us  [body(): scaled = amps / denominator]
    slice x2 -> x3, local copies, waits for them, and re-layouts: 5.92 us -> 7.73 us  [body(): w_cycle[:, s:s + n]]
  transfers between devices with their start and end apart: 5 -> 3, of which waited for: 2 -> 1; matrix products, arithmetic and copies ran while one was open for 1% -> 3% of each run, Pallas kernels for 81% -> 75%
where the time goes in v3:
time: 354 us
  Pallas kernels  287 us (81%)
  waiting for transfers between devices  39.6 us (11%)
  between operations  13.2 us (4%)
  local copies, waits for them, and re-layouts  7.9 us (2%)
  other arithmetic  5.8 us (2%)
    pallas_call x1, Pallas kernels, gather_amps(): pl.pallas_call(gather_kernel, out_shape=jax.ShapeDtypeStruct((js, bs * ro...  149 us
    pallas_call x3, Pallas kernels, product(): pl.pallas_call(functools.partial(product_kernel, first), grid=(columns //...  138 us
    all_gather x3, waiting for transfers between devices, body(): lax.all_gather(w_cycle[:, s:s + n], 'col', axis=0, tiled=True)  39.6 us
    slice x3, local copies, waits for them, and re-layouts, body(): w_cycle[:, s:s + n]  7.73 us
  transfers between devices with their start and end apart: 3, of which 1 were waited for; matrix products, arithmetic and copies ran while one was open for 3% of the time, Pallas kernels for 75%

profile of v3, /device:TPU:0, one launch (start us, length us, event | category | flops | bytes accessed | tf_op | source)
XLA Modules:
  0.0 353.7 jit_solution(2757842096525221532)
XLA Ops:
  6.5 0.0 all-gather.6.cloned.1.call-start
  6.5 3.2 slice.10
  9.7 0.0 all-gather.6.cloned.1.call-update
  9.8 0.0 all-gather.8.cloned.1.call-start
  9.8 2.7 slice.11
  12.5 0.0 all-gather.8.cloned.1.call-update
  12.5 0.0 all-gather.4.cloned.1.call-start
  12.6 1.9 slice.9
  14.4 0.0 all-gather.4.cloned.1.call-update
  14.5 0.0 copy-done
  14.5 0.0 copy-done.1
  14.5 0.2 select_reduce_fusion
  14.7 0.1 dynamic_slice.6
  14.8 0.2 select_reduce_fusion.1
  15.0 0.1 subtract_bitcast_fusion
  15.1 0.1 dynamic_slice.7
  15.2 0.1 broadcast_add_fusion
  15.3 5.2 %subtract_divide_fusion.amps = f32[8,64,2048]{2,1,0:T(8,128)} fusion(f32[8,64,2048]{2,1,0:T(8,128)} %param.7, f32[8]{0:T(128)S(1)} %dynamic_slice.7, f32[64,2048]{1,0:T(8,128)S(1)} %broadcast_add_fusion), kind=kLoop, calls=%fused_computation | loop fusion | flops 2097152 | bytes 8912928 | tf_op jit(solution)/shard_map/div | solution.py:190
  20.4 148.9 %gather_amps.1 = f32[8,512,2048]{2,1,0:T(8,128)} custom-call(f32[8,64,2048]{2,1,0:T(8,128)} %subtract_divide_fusion.amps), custom_call_target="tpu_custom_call" | custom-call | tf_op jit(solution)/shard_map/gather_amps/pallas_call | solution.py:76
  169.4 0.0 all-gather.6.cloned.1.call-done.w
  169.4 68.4 %product.3 = (f32[2048,4096]{1,0:T(8,128)}, bf16[4096,2048]{1,0:T(8,128)(2,1)}, bf16[4096,2048]{1,0:T(8,128)(2,1)}) custom-call(f32[2048,1024]{1,0:T(8,128)} %all-gather.6.cloned.1.call-done.w, f32[4096,2048]{1,0:T(8,128)} %bitcast.4), custom_call_target="tpu_custom_call" | custom-call | flops 51539607552 | bytes 58720256 | tf_op jit(solution)/shard_map/product/pallas_call | solution.py:147
  237.9 39.6 %all-gather.8.cloned.1.call-done.w = f32[2048,768]{1,0:T(8,128)} async-done(((f32[512,768]{1,0:T(8,128)}), f32[2048,768]{1,0:T(8,128)}) %all-gather.8.cloned.1.call-update) | async-done | bytes 6291472 | tf_op jit(solution)/shard_map/all_gather | solution.py:180
  277.4 48.2 %product.4.refs_2_ = f32[2048,4096]{1,0:T(8,128)} custom-call(f32[2048,768]{1,0:T(8,128)} %all-gather.8.cloned.1.call-done.w, bf16[4096,2048]{1,0:T(8,128)(2,1)} %get-tuple-element.8.refs_0_, bf16[4096,2048]{1,0:T(8,128)(2,1)} %get-tuple-element.9.refs_1_, f32[2048,4096]{1,0:T(8,128)} %get-tuple-element.10.refs_2_), custom_call_target="tpu_custom_call", output_to_operand_aliasing={{}: (3, {})} | custom-call | flops 38654705664 | bytes 52428800 | tf_op jit(solution)/shard_map/product/pallas_call | solution.py:147
  325.6 21.6 %product.5 = f32[2048,4096]{1,0:T(8,128)} custom-call(f32[2048,256]{1,0:T(8,128)} %all-gather.4.cloned.1.call-done.w, bf16[4096,2048]{1,0:T(8,128)(2,1)} %get-tuple-element.8.refs_0_, bf16[4096,2048]{1,0:T(8,128)(2,1)} %get-tuple-element.9.refs_1_, f32[2048,4096]{1,0:T(8,128)} %product.4.refs_2_), custom_call_target="tpu_custom_call", output_to_operand_aliasing={{}: (3, {})} | custom-call | flops 12884901888 | bytes 39845888 | tf_op jit(solution)/shard_map/product/pallas_call | solution.py:147
  (8 shorter events, 0.0 us)
Async XLA Ops:
  6.5 162.9 %all-gather.6.cloned.1.call-start = ((), (), s32[]{:S(2)}) async-start(), calls=%async_computation.1 | async-start | bytes 10485760 | tf_op jit(solution)/shard_map/all_gather | solution.py:180
  9.7 4.7 %copy-start = (f32[512]{0:T(512)S(1)}, f32[512]{0:T(512)}, u32[]{:S(2)}) copy-start(f32[512]{0:T(512)} %param.9) | copy-start | bytes 6148
  9.7 4.7 %copy-start.1 = (s32[512]{0:T(512)S(1)}, s32[512]{0:T(512)}, u32[]{:S(2)}) copy-start(s32[512]{0:T(512)} %param.11) | copy-start | bytes 6148
  9.7 5.1 %copy-start.2 = (s32[4]{0:T(128)S(1)}, s32[4]{0:T(128)}, u32[]{:S(2)}) copy-start(s32[4]{0:T(128)} %param.10) | copy-start | bytes 52
  9.7 5.1 %copy-start.3 = (f32[32]{0:T(128)S(1)}, f32[32]{0:T(128)}, u32[]{:S(2)}) copy-start(f32[32]{0:T(128)} %param.8) | copy-start | bytes 388
  9.8 267.7 %all-gather.8.cloned.1.call-start = ((), (), s32[]{:S(2)}) async-start(), calls=%async_computation.2 | async-start | bytes 7864320 | tf_op jit(solution)/shard_map/all_gather | solution.py:180
  12.5 313.1 %all-gather.4.cloned.1.call-start = ((), (), s32[]{:S(2)}) async-start(), calls=%async_computation | async-start | bytes 2621440 | tf_op jit(solution)/shard_map/all_gather | solution.py:180
Sparse Core Ops, SparseCore 0:
  9.9 152.3 all-gather.5
  163.8 113.5 all-gather.7
  279.0 44.1 all-gather.3
